TPU v7x, 512 devices: a whole 4x4x16 slice. The times are simulated.
512 devices in a mesh: row: 32 (over y, x, core), col: 16 (over z).
Axes of the slice: x: 4, y: 4, z: 16, core: 2. Of those that a mesh axis runs over, the one named last changes fastest.
Arguments:
- ainv_block: float32 [4096, 4096], P('row', 'col'), as said below
- factor: float32 [2, 4096, 1024], P(None, 'row', 'col'), may hold values from -0.8 to 0.8
- block_mask: int32 [2, 32], replicated, may hold values 0 or 1
- diag_inverse: float32 [1024, 2, 1024], P('row', None, 'col'), may hold values from -6 to 6
Outputs:
- ainv_panel: float32 [1024, 2, 4096], P('col', None, 'row')
- ainv_diag: float32 [1024, 2, 1024], P('row', None, 'col')
Inputs may be any that keep to these rules, and one draw needn't show every extreme that they name: `ainv_block`: symmetric, diagonal entries between 2 and 3, off-diagonal entries of order one over the square root of 4096.
All inputs are finite; a program needn't handle non-finite values.
Results may differ from a plain program's by a relative error of at most 0.0001.
Values sent between devices are 32-bit elements; how exact they have to be, the bound alone decides.
A program may use at most 64 MiB of HBM per device.

v0:
```python
import jax
import jax.numpy as jnp
from jax import lax
from jax.sharding import PartitionSpec as P

BLOCK = 128


def from_root(block, axis, owner):
    block = jnp.where(lax.axis_index(axis) == owner, block, jnp.zeros_like(block))
    return lax.psum(block, axis)


def local(ainv_block, factor, block_mask, diag_inverse):
    col_count = lax.axis_size("col")
    row_count = lax.axis_size("row")
    ratio = row_count // col_count
    row_index = lax.axis_index("row")
    col_index = lax.axis_index("col")
    rows = factor.shape[1]
    local_blocks = rows // BLOCK
    local_mask = lax.dynamic_slice_in_dim(block_mask, row_index * local_blocks, local_blocks, 1)
    row_mask = jnp.repeat(local_mask, BLOCK, axis=1).astype(jnp.float32)
    masked = factor * row_mask[:, :, None]
    own_rows = lax.all_gather(masked, "col", axis=2, tiled=True)
    pieces = [from_root(own_rows, "row", ratio * col_index + offset) for offset in range(ratio)]
    column_rows = jnp.concatenate(pieces, axis=1)
    piece = column_rows
    summed = lax.psum_scatter(
        jnp.einsum(
            "ij,sjw->wsi",
            ainv_block,
            piece,
            precision=lax.Precision.HIGHEST,
            preferred_element_type=jnp.float32,
        ),
        "col",
        scatter_dimension=0,
        tiled=True,
    )
    ainv_panel = -(summed * row_mask[None, :, :])
    piece = own_rows
    correction = lax.psum_scatter(
        jnp.einsum(
            "siw,vsi->wsv",
            piece,
            ainv_panel,
            precision=lax.Precision.HIGHEST,
            preferred_element_type=jnp.float32,
        ),
        "row",
        scatter_dimension=0,
        tiled=True,
    )
    return (ainv_panel, diag_inverse - correction)


def solution(mesh):
    placed = (P("row", "col"), P(None, "row", "col"), P(), P("row", None, "col"))
    return jax.shard_map(
        local,
        mesh=mesh,
        in_specs=placed,
        out_specs=(P("col", None, "row"), P("row", None, "col")),
        check_vma=False,
    )
```

profile of v0, /device:TPU:1, one launch (start us, length us, event | category | flops | bytes accessed | tf_op | source)
XLA Modules:
  0.0 445.2 jit_solution(8940846543808888751)
XLA Ops:
  7.2 0.0 copy-start
  7.2 0.0 all-gather.2.cloned.1.call-start
  7.2 0.9 convert_reduce_fusion
  8.1 1.5 broadcast_multiply_fusion
  9.6 0.0 all-gather.2.cloned.1.call-update
  9.7 0.0 all-reduce.7.cloned.1.call-start
  9.7 67.8 %all-gather.2.cloned.1.call-done = f32[2,128,1024]{1,2,0:T(8,128)} async-done(((f32[2,128,64]{1,2,0:T(8,128)}), f32[2,128,1024]{1,2,0:T(8,128)}) %all-gather.2.cloned.1.call-update) | async-done | bytes 1048592 | tf_op jit(solution)/shard_map/all_gather | solution.py:25
  77.5 2.7 broadcast_select_fusion.1
  80.2 0.0 all-reduce.7.cloned.1.call-update
  80.3 0.0 reduce-scatter.2.cloned.1.call-start
  80.3 145.2 %all-reduce.7.cloned.1.call-done = (f32[2,128,1024]{1,2,0:T(8,128)}, f32[2,128,1024]{1,2,0:T(8,128)}) async-done(((f32[2,128,1024]{1,2,0:T(8,128)}, f32[2,128,1024]{1,2,0:T(8,128)}), (f32[2,128,1024]{1,2,0:T(8,128)}, f32[2,128,1024]{1,2,0:T(8,128)})) %all-reduce.7.cloned.1.call-update) | async-done | bytes 2097168 | tf_op jit(solution)/shard_map/psum | solution.py:11
  225.5 0.0 copy-done
  225.5 4.3 fusion.4
  229.8 0.0 copy-start.1
  229.8 0.0 reduce-scatter.2.cloned.1.call-update
  229.8 0.0 all-reduce.5.cloned.1.call-start
  229.9 60.2 %reduce-scatter.2.cloned.1.call-done = f32[64,2,128]{2,0,1:T(8,128)} async-done(((f32[1024,2,128]{2,0,1:T(8,128)}), f32[64,2,128]{2,0,1:T(8,128)}) %reduce-scatter.2.cloned.1.call-update) | async-done | bytes 65552 | tf_op jit(solution)/shard_map/reduce_scatter | solution.py:29
  290.1 0.9 multiply_negate_fusion
  291.0 0.0 copy-done.1
  291.0 1.2 convolution_bitcast_fusion
  292.2 0.0 copy-start.2
  292.3 1.3 copy.9
  293.6 0.0 all-reduce.5.cloned.1.call-update
  293.6 1.3 dynamic-slice
  295.5 0.7 copy.10
  296.2 141.0 %all-reduce.5.cloned.1.call-done = f32[1024,2,64]{2,1,0:T(2,128)} async-done(((f32[1024,2,64]{2,1,0:T(2,128)}), f32[1024,2,64]{2,1,0:T(2,128)}) %all-reduce.5.cloned.1.call-update) | async-done | bytes 524304
  437.2 0.0 copy-done.2
  437.2 1.4 dynamic-slice_subtract_fusion
Async XLA Ops:
  7.2 218.3 %copy-start = (f32[128,256]{1,0:T(8,128)S(1)}, f32[128,256]{1,0:T(8,128)}, u32[]{:S(2)}) copy-start(f32[128,256]{1,0:T(8,128)} %param.4) | copy-start | bytes 393220
  7.2 70.4 %all-gather.2.cloned.1.call-start = ((), (), s32[]{:S(2)}) async-start(), calls=%async_computation.1 | async-start | bytes 1114112 | tf_op jit(solution)/shard_map/all_gather | solution.py:25
  9.7 215.8 %all-reduce.7.cloned.1.call-start = ((), (), s32[]{:S(2)}) async-start(), calls=%async_computation.4 | async-start | bytes 4194304 | tf_op jit(solution)/shard_map/psum | solution.py:11
  80.3 209.8 %reduce-scatter.2.cloned.1.call-start = ((), (), s32[]{:S(2)}) async-start(), calls=%async_computation.2 | async-start | bytes 1114112 | tf_op jit(solution)/shard_map/reduce_scatter | solution.py:29
  229.8 61.2 %copy-start.1 = (f32[2,128,1024]{1,2,0:T(8,128)S(1)}, f32[2,128,1024]{1,2,0:T(8,128)}, u32[]{:S(2)}) copy-start(f32[2,128,1024]{1,2,0:T(8,128)} %all-gather.2.cloned.1.call-done) | copy-start | bytes 3145732
  229.8 207.4 %all-reduce.5.cloned.1.call-start = ((), (), s32[]{:S(2)}) async-start(), calls=%async_computation.3 | async-start | bytes 2097152
  292.2 145.0 %copy-start.2 = (f32[32,2,64]{2,1,0:T(2,128)S(1)}, f32[32,2,64]{2,1,0:T(2,128)}, u32[]{:S(2)}) copy-start(f32[32,2,64]{2,1,0:T(2,128)} %param.7) | copy-start | bytes 49156
Sparse Core Ops, SparseCore 0:
  10.7 66.8 all-gather.1
  80.8 144.5 all-reduce.6
  230.0 60.0 reduce-scatter.1
  293.7 143.4 all-reduce.4
where the time goes:
time: 446 us; the launch traced here: 445 us
  waiting for transfers between devices  414 us (93%)
  between operations  14.5 us (3%)
  other arithmetic  7.42 us (2%)
  matrix products  5.58 us (1%)
    psum x1, waiting for transfers between devices, from_root(): return lax.psum(block, axis)  145 us
    unnamed x5, waiting for transfers between devices  141 us
    all_gather x1, waiting for transfers between devices, local(): own_rows = lax.all_gather(masked, 'col', axis=2, tiled=True)  67.8 us
    reduce_scatter x1, waiting for transfers between devices, local(): lax.psum_scatter(jnp.einsum('ij,sjw->wsi', ainv_block, piece, precision=l...  60.2 us
  transfers between devices with their start and end apart: 4, of which 4 were waited for; matrix products, arithmetic and copies ran while one was open for 0% of the time, Pallas kernels for 0%

commit v1 on v0

--- a/solution.py
+++ b/solution.py
@@ -22,7 +22,9 @@
     local_mask = lax.dynamic_slice_in_dim(block_mask, row_index * local_blocks, local_blocks, 1)
     row_mask = jnp.repeat(local_mask, BLOCK, axis=1).astype(jnp.float32)
     masked = factor * row_mask[:, :, None]
-    own_rows = lax.all_gather(masked, "col", axis=2, tiled=True)
+    own_rows = jnp.concatenate(
+        lax.all_to_all(jnp.stack([masked] * lax.axis_size("col")), "col", 0, 0), axis=2
+    )
     pieces = [from_root(own_rows, "row", ratio * col_index + offset) for offset in range(ratio)]
     column_rows = jnp.concatenate(pieces, axis=1)
     piece = column_rows

time: 446 us -> 433 us (0.971)
  waiting for transfers between devices: 414 us -> 387 us
  starting transfers between devices: 0.16 us -> 15.9 us
    all_gather x1 -> x0, waiting for transfers between devices: 67.8 us -> none  [local(): own_rows = lax.all_gather(masked, 'col', axis=2, tiled=True)]
    all_to_all x0 -> x1, waiting for transfers between devices: none -> 44.8 us  [local(): lax.all_to_all(jnp.stack([masked] * lax.axis_size('col')), 'col', 0, 0)]
    all_to_all x0 -> x1, starting transfers between devices: none -> 15.7 us  [local(): lax.all_to_all(jnp.stack([masked] * lax.axis_size('col')), 'col', 0, 0)]
    unnamed x5 -> x4, waiting for transfers between devices: 141 us -> 141 us
where the time goes in v1:
time: 433 us
  waiting for transfers between devices  387 us (89%)
  starting transfers between devices  15.9 us (4%)
  between operations  14.5 us (3%)
  matrix products  5.58 us (1%)
  other arithmetic  5.57 us (1%)
  local copies, waits for them, and re-layouts  4.42 us (1%)
    unnamed x4, waiting for transfers between devices  141 us
    psum x1, waiting for transfers between devices, from_root(): return lax.psum(block, axis)  141 us
    reduce_scatter x1, waiting for transfers between devices, local(): lax.psum_scatter(jnp.einsum('ij,sjw->wsi', ainv_block, piece, precision=l...  60.2 us
    all_to_all x1, waiting for transfers between devices, local(): lax.all_to_all(jnp.stack([masked] * lax.axis_size('col')), 'col', 0, 0)  44.8 us
    all_to_all x1, starting transfers between devices, local(): lax.all_to_all(jnp.stack([masked] * lax.axis_size('col')), 'col', 0, 0)  15.7 us
  transfers between devices with their start and end apart: 4, of which 4 were waited for; matrix products, arithmetic and copies ran while one was open for 0% of the time, Pallas kernels for 0%

profile of v1, /device:TPU:1, one launch (start us, length us, event | category | flops | bytes accessed | tf_op | source)
XLA Modules:
  0.0 432.8 jit_solution(13041733305921323470)
XLA Ops:
  7.2 0.0 copy-start
  7.2 0.9 convert_reduce_fusion
  8.1 0.9 broadcast_multiply_fusion
  9.0 1.1 stack.2
  10.1 15.7 %all-to-all-start = ((f32[16,2,128,64]{2,3,1,0:T(8,128)}), f32[16,2,128,64]{2,3,1,0:T(8,128)S(1)}, u32[]{:S(2)}, u32[]{:S(2)}) async-start(f32[16,2,128,64]{2,3,1,0:T(8,128)} %stack.2), calls=%async_computation | async-start | bytes 2097152 | tf_op jit(solution)/shard_map/all_to_all | solution.py:26
  25.8 0.0 all-reduce.7.cloned.1.call-start
  25.9 44.8 %all-to-all-done = f32[16,2,128,64]{2,3,1,0:T(8,128)S(1)} async-done(((f32[16,2,128,64]{2,3,1,0:T(8,128)}), f32[16,2,128,64]{2,3,1,0:T(8,128)S(1)}, u32[]{:S(2)}, u32[]{:S(2)}) %all-to-all-start) | async-done | bytes 1048608 | tf_op jit(solution)/shard_map/all_to_all | solution.py:26
  70.7 0.1 copy.10
  70.8 1.4 broadcast_select_fusion.1
  72.2 0.0 all-reduce.7.cloned.1.call-update
  72.3 0.0 reduce-scatter.2.cloned.1.call-start
  72.3 140.8 %all-reduce.7.cloned.1.call-done = (f32[2,128,1024]{1,2,0:T(8,128)}, f32[2,128,1024]{1,2,0:T(8,128)}) async-done(((f32[2,128,1024]{1,2,0:T(8,128)}, f32[2,128,1024]{1,2,0:T(8,128)}), (f32[2,128,1024]{1,2,0:T(8,128)}, f32[2,128,1024]{1,2,0:T(8,128)})) %all-reduce.7.cloned.1.call-update) | async-done | bytes 2097168 | tf_op jit(solution)/shard_map/psum | solution.py:11
  213.1 0.0 copy-done
  213.1 4.3 %fusion.4 = f32[1024,2,128]{2,0,1:T(8,128)} fusion(f32[2,128,1024]{1,2,0:T(8,128)} %get-tuple-element.6, f32[2,128,1024]{1,2,0:T(8,128)} %get-tuple-element.7, f32[128,256]{1,0:T(8,128)S(1)} %copy-done), kind=kOutput, calls=%fused_computation.4 | convolution fusion | flops 805830656 | bytes 3276800 | tf_op jit(solution)/shard_map/ij,sjw->wsi/dot_general | solution.py:32
  217.5 0.0 reduce-scatter.2.cloned.1.call-update
  217.5 0.0 all-reduce.5.cloned.1.call-start
  217.6 60.2 %reduce-scatter.2.cloned.1.call-done = f32[64,2,128]{2,0,1:T(8,128)} async-done(((f32[1024,2,128]{2,0,1:T(8,128)}), f32[64,2,128]{2,0,1:T(8,128)}) %reduce-scatter.2.cloned.1.call-update) | async-done | bytes 65552 | tf_op jit(solution)/shard_map/reduce_scatter | solution.py:31
  277.8 0.9 multiply_negate_fusion
  278.7 1.2 convolution_bitcast_fusion
  280.0 0.0 copy-start.1
  280.0 1.3 copy.12
  281.2 0.0 all-reduce.5.cloned.1.call-update
  281.3 1.3 dynamic-slice
  283.2 0.7 copy.13
  283.9 141.0 %all-reduce.5.cloned.1.call-done = f32[1024,2,64]{2,1,0:T(2,128)} async-done(((f32[1024,2,64]{2,1,0:T(2,128)}), f32[1024,2,64]{2,1,0:T(2,128)}) %all-reduce.5.cloned.1.call-update) | async-done | bytes 524304
  424.9 0.0 copy-done.1
  424.9 1.4 dynamic-slice_subtract_fusion
Async XLA Ops:
  7.2 206.0 %copy-start = (f32[128,256]{1,0:T(8,128)S(1)}, f32[128,256]{1,0:T(8,128)}, u32[]{:S(2)}) copy-start(f32[128,256]{1,0:T(8,128)} %param.4) | copy-start | bytes 393220
  10.1 60.6 %all-to-all-start = ((f32[16,2,128,64]{2,3,1,0:T(8,128)}), f32[16,2,128,64]{2,3,1,0:T(8,128)S(1)}, u32[]{:S(2)}, u32[]{:S(2)}) async-start(f32[16,2,128,64]{2,3,1,0:T(8,128)} %stack.2), calls=%async_computation | async-start | bytes 2097152 | tf_op jit(solution)/shard_map/all_to_all | solution.py:26
  25.8 187.3 %all-reduce.7.cloned.1.call-start = ((), (), s32[]{:S(2)}) async-start(), calls=%async_computation.4 | async-start | bytes 4194304 | tf_op jit(solution)/shard_map/psum | solution.py:11
  72.3 205.5 %reduce-scatter.2.cloned.1.call-start = ((), (), s32[]{:S(2)}) async-start(), calls=%async_computation.2 | async-start | bytes 1114112 | tf_op jit(solution)/shard_map/reduce_scatter | solution.py:31
  217.5 207.4 %all-reduce.5.cloned.1.call-start = ((), (), s32[]{:S(2)}) async-start(), calls=%async_computation.3 | async-start | bytes 2097152
  280.0 144.9 %copy-start.1 = (f32[32,2,64]{2,1,0:T(2,128)S(1)}, f32[32,2,64]{2,1,0:T(2,128)}, u32[]{:S(2)}) copy-start(f32[32,2,64]{2,1,0:T(2,128)} %param.7) | copy-start | bytes 49156
Sparse Core Ops, SparseCore 0:
  72.4 140.7 all-reduce.6
  217.6 60.1 reduce-scatter.1
  281.4 143.4 all-reduce.4
